TPU v7x, 512 devices: a whole 4x8x8 slice. The times are simulated.
512 devices in a mesh: stream: 64 (over y, z), span: 8 (over x, core).
Axes of the slice: x: 4, y: 8, z: 8, core: 2. Of those that a mesh axis runs over, the one named last changes fastest.
Arguments:
- solution: float32 [80, 4, 128, 8, 128], P(None, None, 'stream', 'span'), may hold values from -6 to 6
- forcing: float32 [80, 4, 128, 8, 128], P(None, None, 'stream', 'span'), may hold values from -6 to 6
- pseudo_shift: float32 [128, 8, 128], P('stream', 'span'), may hold values from 0.02 to 0.2
- stream_faces: float32 [128, 8, 128], P('stream', 'span'), may hold values from 5 to 50
- span_faces: float32 [128, 8, 128], P('stream', 'span'), may hold values from 0.05 to 0.5
- normal_faces: float32 [128, 8, 128], P('stream', 'span'), may hold values from 0.05 to 0.5
- coupling_span: float32 [80, 80], replicated, may hold values from -0.625 to 0.625
- coupling_normal: float32 [80, 80], replicated, may hold values from -0.625 to 0.625
- reflectors: float32 [8, 80], replicated, may hold values from -6 to 6
- eigenvalues: float32 [80], replicated, may hold values from -1 to 1
- line_start: int32 [8, 128], P('span'), may hold values from 0 to 112, as said below
- line_length: int32 [8, 128], P('span'), may hold values from 16 to 128
- line_order: int32 [8, 128], P('span'), may hold values from 0 to 127, each once within a row
Outputs:
- relaxed: float32 [80, 4, 128, 8, 128], P(None, None, 'stream', 'span')
- line_states: float32 [80, 4, 1024, 128], P(None, None, ('span', 'stream'))
Inputs may be any that keep to these rules, and one draw needn't show every extreme that they name: Each line ends inside the grid: line_start + line_length <= 128. `line_order`: each row lists every line of its spanwise tile once; slot j belongs to the stream device j // 2.
All inputs are finite; a program needn't handle non-finite values.
Results may differ from a plain program's by a relative error of at most 0.0003.
Values sent between devices are 32-bit elements; how exact they have to be, the bound alone decides.
A program may use at most 128 MiB of HBM per device.

v0:
```python
import functools

import jax
import jax.numpy as jnp
from jax import lax
from jax.experimental import pallas as pl
from jax.experimental.pallas import tpu as pltpu
from jax.sharding import PartitionSpec as P

F32 = jnp.float32
BF16 = jnp.bfloat16
MESH = pl.DeviceIdType.MESH
EPS = 1e-06


def iota(shape, dim):
    return lax.broadcasted_iota(jnp.int32, shape, dim)


def split(x):
    high = x.astype(BF16)
    return high, (x - high.astype(F32)).astype(BF16)


def split3(x):
    high = x.astype(BF16)
    rest = x - high.astype(F32)
    mid = rest.astype(BF16)
    return high, mid, (rest - mid.astype(F32)).astype(BF16)


def dot(a, b, ca=1, cb=0):
    return lax.dot_general(a, b, (((ca,), (cb,)), ((), ())), preferred_element_type=F32)


def dot3(a, b, ca=1, cb=0):
    ah, al = split(a)
    bh, bl = split(b)
    return dot(ah, bh, ca, cb) + (dot(al, bh, ca, cb) + dot(ah, bl, ca, cb))


def body(
    sol, frc, pse, stf, spf, nof, cs, cn, reflectors, lam, start, length, order,
    out_rel, out_ls,
    pse_ref, stf_ref, nof_ref, cs_ref, cn_ref, refl_ref, lam_ref, start_ref, length_ref, order_ref,
    u_buf, ul_buf, ur_buf, f_buf, spf_send, spl_recv, m2_send, m2l_recv, m2r_recv,
    e_send, e_recv, g_send, g_recv, y_send, y_recv,
    pad_buf, da_buf, db_buf, f0_buf, f1_buf, inv_buf, a_buf, b_buf, d_buf, rel_buf, ls_buf,
    loc_sem, out_sem, halo_send_sem, halo_recv_sem, tiny_send_sem, tiny_recv_sem,
    e_sems, gs_sem, gr_sem, ys_sem, yr_sem,
):
    me = lax.axis_index("stream")
    count = lax.axis_size("stream")
    sp = lax.axis_index("span")
    sp_count = lax.axis_size("span")
    sp_left = lax.rem(sp + sp_count - 1, sp_count)
    sp_right = lax.rem(sp + 1, sp_count)
    st_left = lax.rem(me + count - 1, count)
    st_right = lax.rem(me + 1, count)

    loads_u = [
        pltpu.make_async_copy(sol.at[:, rs // 2, rs % 2, 0, :], u_buf.at[rs], loc_sem.at[rs]) for rs in range(8)
    ]
    loads_f = [
        pltpu.make_async_copy(frc.at[:, rs // 2, rs % 2, 0, :], f_buf.at[rs], loc_sem.at[8 + rs]) for rs in range(8)
    ]
    first = ((order, order_ref), (spf.at[:, 0], spf_send), (reflectors, refl_ref), (lam, lam_ref))
    later = (
        (cs, cs_ref), (cn, cn_ref), (pse.at[:, 0], pse_ref), (stf.at[:, 0], stf_ref), (nof.at[:, 0], nof_ref),
        (start, start_ref), (length, length_ref),
    )
    loads_small = [
        pltpu.make_async_copy(src, dst, loc_sem.at[16 + i]) for i, (src, dst) in enumerate(first + later)
    ]
    for load in loads_small[:4]:
        load.start()
    for load in loads_u:
        load.start()
    for load in loads_small[4:]:
        load.start()
    for load in loads_f:
        load.start()
    g_recv[...] = jnp.zeros_like(g_recv)

    barrier = pltpu.get_barrier_semaphore()
    for side in (sp_left, sp_right):
        pl.semaphore_signal(barrier, inc=1, device_id={"span": side}, device_id_type=MESH)

    def greet(i, carry):
        pl.semaphore_signal(
            barrier, inc=1, device_id={"stream": lax.rem(me + i, count)}, device_id_type=MESH
        )
        return carry

    lax.fori_loop(1, count, greet, 0)

    for load in loads_small[:4]:
        load.wait()

    lane = iota((128, 128), 1)
    row = iota((128, 128), 0)
    perm_t = jnp.where(row == order_ref[...], 1.0, 0.0).astype(BF16)
    pair_line = row // 64
    pick = jnp.where(lane == 2 * (row - 64 * pair_line) + pair_line, 1.0, 0.0).astype(BF16)
    perm = dot(pick, perm_t, 1, 1).astype(BF16)

    for load in loads_u:
        load.wait()
    pl.semaphore_wait(barrier, count + 1)

    halos = []
    for c in range(2):
        for k, (side, buf) in enumerate(((sp_right, ul_buf), (sp_left, ur_buf))):
            halo = pltpu.make_async_remote_copy(
                u_buf.at[pl.ds(4 * c, 4)],
                buf.at[pl.ds(4 * c, 4)],
                halo_send_sem.at[2 * c + k],
                halo_recv_sem.at[2 * c + k],
                device_id={"span": side},
                device_id_type=MESH,
            )
            if c == 0 and k == 0:
                spf_halo = pltpu.make_async_remote_copy(
                    spf_send, spl_recv, tiny_send_sem.at[0], tiny_recv_sem.at[0],
                    device_id={"span": sp_right}, device_id_type=MESH,
                )
                spf_halo.start()
            halo.start()
            halos.append(halo)

    for load in loads_small[4:]:
        load.wait()

    pad_buf[...] = jnp.zeros_like(pad_buf)
    pad_buf[0:8, 0:80] = refl_ref[...]
    pad_buf[8:9, 0:80] = lam_ref[...]
    refl = pad_buf[0:8, :]
    lam_row = pad_buf[8:9, :]
    norms = jnp.sum(refl * refl, axis=1, keepdims=True)
    factors = 2.0 / (norms + EPS)
    scales = 2.0 * (EPS**0.5) / (norms + EPS)
    lane80 = iota((80, 128), 1)
    row8 = iota((8, 128), 0)
    basis = jnp.where(iota((80, 128), 0) == lane80, 1.0, 0.0)
    side_z = jnp.zeros((80, 128), F32)
    side_p = jnp.zeros((8, 128), F32)
    for k in range(8):
        w = refl[k : k + 1, :]
        factor = factors[k : k + 1, :]
        z = jnp.sum(basis * w, axis=1, keepdims=True)
        basis = basis - (factor * z) * w
        side_z = jnp.where(lane80 == 80 + k, z * scales[k : k + 1, :], side_z)
        side_p = side_p - (factor * jnp.sum(side_p * w, axis=1, keepdims=True)) * w
        side_p = jnp.where(row8 == k, w, side_p)
    side_p = side_p * scales
    basis_z = basis + side_z
    zt = jnp.transpose(jnp.concatenate([basis_z, jnp.zeros((48, 128), F32)], axis=0))[80:88, 0:80]
    m1 = dot3(side_p * jnp.abs(lam_row), basis, 1, 1)
    m2 = dot3(side_p * lam_row, basis, 1, 1)
    small = jnp.concatenate([m1, m2, zt], axis=0)
    state = jnp.concatenate([u_buf[rs] for rs in range(8)], axis=1)
    small_u = dot3(small, state)

    def part(base, r, s):
        rs = 2 * r + s
        return small_u[base : base + 8, rs * 128 : rs * 128 + 128]

    for s in range(2):
        for r in range(4):
            m2_send[s, 8 * r : 8 * r + 8, :] = part(8, r, s)
        m2_send[s, 32:40, :] = jnp.broadcast_to(stf_ref[s : s + 1, :], (8, 128))
    m2_halos = [
        pltpu.make_async_remote_copy(
            m2_send.at[1 - k], buf, tiny_send_sem.at[1 + k], tiny_recv_sem.at[1 + k],
            device_id={"stream": side}, device_id_type=MESH,
        )
        for k, (side, buf) in enumerate(((st_right, m2l_recv), (st_left, m2r_recv)))
    ]
    for halo in m2_halos:
        halo.start()

    line_start = start_ref[...]
    line_end = line_start + length_ref[...]

    def masked(faces, pos):
        return jnp.where((pos >= line_start) & (pos + 1 < line_end), faces, 0.0)

    face = [masked(stf_ref[s : s + 1, :], 2 * me + s) for s in range(2)]
    lane1 = iota((1, 128), 1)
    normal_face = [jnp.where(lane1 < 127, nof_ref[s : s + 1, :], 0.0) for s in range(2)]
    normal_left = [jnp.where(lane1 > 0, pltpu.roll(normal_face[s], 1, 1), 0.0) for s in range(2)]
    span_face = [spf_send[s : s + 1, :] for s in range(2)]
    spf_halo.wait_recv()
    span_left = [spl_recv[s : s + 1, :] for s in range(2)]
    diag = [
        pse_ref[s : s + 1, :] + span_left[s] + span_face[s] + normal_left[s] + normal_face[s]
        for s in range(2)
    ]

    lane64 = iota((64, 128), 1)
    first_line = ((lane64 // 32) % 2) == 0
    low_half = lane64 < 64
    perm2 = jnp.concatenate([perm, perm], axis=1)
    perm3 = jnp.concatenate([perm, perm, perm], axis=1)
    h_rows = jnp.concatenate([part(16, r, s) for s in range(2) for l in range(2) for r in range(4)], axis=0)
    c_rows = jnp.concatenate(
        [
            jnp.broadcast_to((diag, face)[q][s], (16, 128))
            for s in range(2)
            for l in range(2)
            for q in range(2)
        ],
        axis=0,
    )
    e_flat = e_send.reshape(64 * 8, 128)
    by_slot = dot(perm2, jnp.concatenate(split(h_rows), axis=1), 1, 1)
    e_flat[pl.ds(0, 64, stride=8), :] = jnp.where(first_line, by_slot[:64], by_slot[64:])
    by_slot = dot(perm3, jnp.concatenate(split3(c_rows), axis=1), 1, 1)
    e_flat[pl.ds(1, 64, stride=8), :] = jnp.where(first_line, by_slot[:64], by_slot[64:])

    def send_all(src, dst, rows, send_sem, recv_sem):
        def one(i, carry):
            peer = lax.rem(me + i, count)
            pltpu.make_async_remote_copy(
                src.at[peer, pl.ds(0, rows)],
                dst.at[me, pl.ds(0, rows)],
                send_sem,
                recv_sem,
                device_id={"stream": peer},
                device_id_type=MESH,
            ).start()
            return carry

        lax.fori_loop(1, count, one, 0)

    def wait_all(buf, rows, sem):
        blocks = buf.at[pl.ds(0, 63), pl.ds(0, rows)]
        pltpu.make_async_copy(blocks, blocks, sem).wait()

    send_all(e_send, e_recv, 2, e_sems.at[0], e_sems.at[1])
    e_recv[me] = e_send[me]

    weights_t = jnp.concatenate(
        [basis, dot3(cs_ref[...], basis, 0, 0), dot3(cn_ref[...], basis, 0, 0), side_p, jnp.zeros((8, 128), F32)],
        axis=0,
    )
    weights = jnp.transpose(weights_t)[:80]
    weights_high, weights_low = split(weights)
    weights_both = jnp.concatenate([weights_high, weights_low], axis=0)
    for load in loads_f:
        load.wait()
    for halo in m2_halos:
        halo.wait_recv()
    face_left = [masked(m2l_recv[32:33, :], 2 * me - 1), face[0]]

    for c in range(2):
        halos[2 * c].wait_recv()
        halos[2 * c + 1].wait_recv()
        columns = []
        for r in (2 * c, 2 * c + 1):
            for s in range(2):
                rs = 2 * r + s
                u = u_buf[rs]
                before = m2l_recv[8 * r : 8 * r + 8, :] if s == 0 else part(8, r, 0)
                after = part(8, r, 1) if s == 0 else m2r_recv[8 * r : 8 * r + 8, :]
                columns.append(
                    jnp.concatenate(
                        [
                            f_buf[rs],
                            span_left[s] * ul_buf[rs] + span_face[s] * ur_buf[rs],
                            normal_left[s] * pltpu.roll(u, 1, 1) + normal_face[s] * pltpu.roll(u, 127, 1),
                            (face_left[s] + face[s]) * part(0, r, s) - face_left[s] * before - face[s] * after,
                            jnp.zeros((8, 128), F32),
                        ],
                        axis=0,
                    )
                )
        high, low = split(jnp.concatenate(columns, axis=1))
        both = dot(weights_both, high)
        modal = both[:80] + (both[80:] + dot(weights_high, low))
        modal_high, modal_low = split(modal)
        g_flat = g_send.at[c].reshape(64 * 8, 128)
        for kg in range(5):
            rows = [
                jnp.concatenate(
                    [
                        half[kg * 16 : kg * 16 + 16, (2 * r + s) * 128 : (2 * r + s) * 128 + 128]
                        for s in range(2)
                        for l in range(2)
                        for r in range(2)
                    ],
                    axis=0,
                )
                for half in (modal_high, modal_low)
            ]
            by_slot = dot(perm2, jnp.concatenate(rows, axis=1), 1, 1)
            g_flat[pl.ds(kg, 64, stride=8), :] = jnp.where(first_line, by_slot[:64], by_slot[64:])
        send_all(g_send.at[c], g_recv.at[c], 5, gs_sem.at[c], gr_sem.at[c])
        g_recv[c, me] = g_send[c, me]

    lam_groups = jnp.where((iota((8, 128), 1) // 16) == row8, lam_row, 0.0)
    spread = jnp.where((row % 16) == (lane % 16), 1.0, 0.0).astype(BF16)
    lam_h, lam_m, lam_l = split3(lam_groups)
    rate = dot(lam_h, spread) + dot(lam_m, spread) + dot(lam_l, spread)
    rate_abs = jnp.abs(rate)
    wait_all(e_recv, 2, e_sems.at[1])
    e_got = e_recv.reshape(64 * 8, 128)
    coeffs = e_got[pl.ds(1, 64, stride=8), :]
    even_group = ((lane64 // 16) % 2) == 0
    d_both = jnp.where(even_group, coeffs, pltpu.roll(coeffs, 16, 1))
    f_both = jnp.where(even_group, pltpu.roll(coeffs, 112, 1), coeffs)
    f_swap = pltpu.roll(f_both, 64, 1)
    da_buf[...] = d_both
    db_buf[...] = pltpu.roll(d_both, 64, 1)
    f0_buf[...] = jnp.where(low_half, f_both, f_swap)
    f1_buf[0:8, :] = jnp.zeros((8, 128), F32)
    f1_buf[pl.ds(8, 64), :] = jnp.where(low_half, f_swap, f_both)
    low1 = lane1 < 64
    low8 = iota((8, 128), 1) < 64

    def factor_step(t, d_row, f_now, f_next, inv_before):
        x = rate * f_now
        main = d_row + rate_abs * (f_now + f_next)
        inv = 1.0 / (main - x * x * inv_before)
        inv_buf[t] = inv
        a_buf[t] = x * inv
        b_buf[t] = rate * f_next * inv
        return inv

    def factor(p, inv):
        q = 63 - p
        f_0 = jnp.where(low1, f1_buf[pl.ds(p + 7, 1), :], f1_buf[pl.ds(q + 8, 1), :])
        f_1 = jnp.where(low1, f0_buf[pl.ds(p, 1), :], f0_buf[pl.ds(q, 1), :])
        f_2 = jnp.where(low1, f1_buf[pl.ds(p + 8, 1), :], f1_buf[pl.ds(q + 7, 1), :])
        d_0 = jnp.where(low1, da_buf[pl.ds(p, 1), :], da_buf[pl.ds(q, 1), :])
        d_1 = jnp.where(low1, db_buf[pl.ds(p, 1), :], db_buf[pl.ds(q, 1), :])
        inv = factor_step(2 * p, d_0, f_0, f_1, inv)
        return factor_step(2 * p + 1, d_1, f_1, f_2, inv)

    lax.fori_loop(0, 32, factor, jnp.zeros((8, 128), F32))
    b_last = b_buf[63]
    middle = 1.0 / (1.0 - b_last * pltpu.roll(b_last, 64, 1))

    def turned(rows):
        high = rows.astype(BF16).astype(F32)
        return jnp.transpose(jnp.concatenate([high, rows - high], axis=0)).astype(BF16)

    owner = row - 64 * pair_line
    to_cell = jnp.concatenate(
        [jnp.where(lane == 2 * owner + s, 1.0, 0.0).astype(BF16) for s in range(2)], axis=0
    )
    to_normal = jnp.concatenate([perm[:64], perm[:64], perm[64:], perm[64:]], axis=0)
    h_turned = turned(e_got[pl.ds(0, 64, stride=8), :])
    h_own = dot(jnp.concatenate([h_turned[:64], h_turned[64:]], axis=1), to_cell)
    basis_88 = basis_z[:, 0:88]
    basis_high, basis_low = split(basis_88)
    basis_both = jnp.concatenate([basis_high, basis_low], axis=0)

    def leave_modes(flat, select, lines, side_rows):
        pieces = []
        for kg in range(5):
            t = turned(flat[pl.ds(kg, 64, stride=8), :])
            if lines:
                pair = (jnp.concatenate([t[0:32], t[64:96]], axis=0), jnp.concatenate([t[32:64], t[96:128]], axis=0))
            else:
                pair = (t[:64], t[64:])
            pieces.append(jnp.concatenate(pair, axis=1))
        moved = dot(jnp.concatenate(pieces, axis=0), select)
        columns = [
            jnp.concatenate(
                [moved[kg * 64 + x * 32 + r * 16 : kg * 64 + x * 32 + r * 16 + 16] for kg in range(5)]
                + [side_rows(x, r)],
                axis=0,
            )
            for r in range(2)
            for x in range(2)
        ]
        high, low = split(jnp.concatenate(columns, axis=1))
        both = dot(basis_both, high)
        return both[:80] + (both[80:] + dot(basis_high, low))

    stores = []
    for c in range(2):
        wait_all(g_recv.at[c], 5, gr_sem.at[c])

        def forward(p, d, c=c):
            near = g_recv[c, p]
            far = g_recv[c, 63 - p]
            d = inv_buf[2 * p] * jnp.where(low8, near, far) + a_buf[2 * p] * d
            d_buf[2 * p] = d
            odd = pltpu.roll(jnp.where(low8, far, near), 64, 1)
            d = inv_buf[2 * p + 1] * odd + a_buf[2 * p + 1] * d
            d_buf[2 * p + 1] = d
            return d

        d = lax.fori_loop(0, 32, forward, jnp.zeros((8, 128), F32))
        y = (d + b_last * pltpu.roll(d, 64, 1)) * middle

        def backward(i, y, c=c):
            p = 31 - i
            y_odd = d_buf[2 * p + 1] + b_buf[2 * p + 1] * y
            y_even = d_buf[2 * p] + b_buf[2 * p] * y_odd
            swapped = pltpu.roll(y_odd, 64, 1)
            y_send[c, p] = jnp.where(low8, y_even, swapped)
            y_send[c, 63 - p] = jnp.where(low8, swapped, y_even)
            return y_even

        lax.fori_loop(0, 32, backward, pltpu.roll(y, 64, 1))
        send_all(y_send.at[c], y_recv.at[c], 5, ys_sem.at[c], yr_sem.at[c])
        y_recv[c, me] = y_send[c, me]
        left = leave_modes(
            y_send.at[c].reshape(64 * 8, 128),
            to_cell,
            False,
            lambda x, r, c=c: h_own[x * 32 + (2 * c + r) * 8 : x * 32 + (2 * c + r) * 8 + 8],
        )
        for r in range(2):
            for x in range(2):
                at = (2 * c + r) * 2 + x
                ls_buf[at] = left[:, (2 * r + x) * 128 : (2 * r + x) * 128 + 128]
                stores.append(
                    pltpu.make_async_copy(ls_buf.at[at], out_ls.at[:, 2 * c + r, x, 0, :], out_sem.at[at])
                )
                stores[-1].start()
    for c in range(2):
        wait_all(y_recv.at[c], 5, yr_sem.at[c])
        left = leave_modes(
            y_recv.at[c].reshape(64 * 8, 128), to_normal, True, lambda x, r, c=c: part(16, 2 * c + r, x)
        )
        for r in range(2):
            for x in range(2):
                at = (2 * c + r) * 2 + x
                rel_buf[at] = left[:, (2 * r + x) * 128 : (2 * r + x) * 128 + 128]
                stores.append(
                    pltpu.make_async_copy(rel_buf.at[at], out_rel.at[:, 2 * c + r, x, 0, :], out_sem.at[8 + at])
                )
                stores[-1].start()

    spf_halo.wait_send()
    for halo in m2_halos:
        halo.wait_send()
    for halo in halos:
        halo.wait_send()
    wait_all(e_send, 2, e_sems.at[0])
    for c in range(2):
        wait_all(g_send.at[c], 5, gs_sem.at[c])
        wait_all(y_send.at[c], 5, ys_sem.at[c])
    for store in stores:
        store.wait()


def per_device(
    solution, forcing, pseudo_shift, stream_faces, span_faces, normal_faces, coupling_span, coupling_normal,
    reflectors, eigenvalues, line_start, line_length, line_order,
):
    hbm = pl.BlockSpec(memory_space=pltpu.HBM)
    block = pltpu.VMEM((8, 80, 128), F32)
    per_peer = pltpu.VMEM((64, 8, 128), F32)
    pair_per_peer = pltpu.VMEM((2, 64, 8, 128), F32)
    two = pltpu.VMEM((2, 128), F32)
    line = pltpu.VMEM((1, 128), jnp.int32)
    dma = pltpu.SemaphoreType.DMA
    out = jax.ShapeDtypeStruct((80, 4, 2, 1, 128), F32)
    relaxed, line_states = pl.pallas_call(
        body,
        out_shape=(out, out),
        in_specs=[hbm] * 13,
        out_specs=(hbm, hbm),
        scratch_shapes=[
            two, two, two, pltpu.VMEM((80, 80), F32), pltpu.VMEM((80, 80), F32),
            pltpu.VMEM((8, 80), F32), pltpu.VMEM((1, 80), F32), line, line, line,
            block, block, block, block,
            two, two,
            pltpu.VMEM((2, 40, 128), F32), pltpu.VMEM((40, 128), F32), pltpu.VMEM((40, 128), F32),
            per_peer, per_peer, pair_per_peer, pair_per_peer, pair_per_peer, pair_per_peer,
            pltpu.VMEM((16, 128), F32),
            pltpu.VMEM((64, 128), F32), pltpu.VMEM((64, 128), F32), pltpu.VMEM((64, 128), F32), pltpu.VMEM((72, 128), F32),
            per_peer, per_peer, per_peer, per_peer, block, block,
            dma((27,)), dma((16,)), dma((4,)), dma((4,)), dma((3,)), dma((3,)),
            dma((2,)), dma((2,)), dma((2,)), dma((2,)), dma((2,)),
        ],
        compiler_params=pltpu.CompilerParams(
            collective_id=0, has_side_effects=True, vmem_limit_bytes=63 << 20
        ),
        name="relax",
    )(
        solution, forcing, pseudo_shift, stream_faces, span_faces, normal_faces,
        coupling_span, coupling_normal, reflectors, eigenvalues.reshape(1, 80), line_start, line_length, line_order,
    )
    return relaxed, line_states.reshape(80, 4, 2, 128)


def solution(mesh):
    cells = P(None, None, "stream", "span", None)
    weights = P("stream", "span", None)
    tiles = P("span", None)
    return jax.shard_map(
        per_device,
        mesh=mesh,
        in_specs=(cells, cells, weights, weights, weights, weights, P(), P(), P(), P(), tiles, tiles, tiles),
        out_specs=(cells, P(None, None, ("span", "stream"), None)),
        check_vma=False,
    )
```

profile of v0, /device:TPU:2, one launch (start us, length us, event | category | flops | bytes accessed | tf_op | source)
XLA Modules:
  0.0 55.7 jit_solution(5265940071086914861)
XLA Ops:
  0.6 52.3 %relax.1 = (f32[80,4,2,1,128]{4,3,2,1,0:T(1,128)}, f32[80,4,2,1,128]{4,3,2,1,0:T(1,128)}) custom-call(f32[80,4,2,1,128]{4,3,2,1,0:T(1,128)} %sol.1, f32[80,4,2,1,128]{4,3,2,1,0:T(1,128)} %frc.1, f32[2,1,128]{2,1,0:T(1,128)} %pse.1, f32[2,1,128]{2,1,0:T(1,128)} %stf.1, f32[2,1,128]{2,1,0:T(1,128)} %spf.1, f32[2,1,128]{2,1,0:T(1,128)} %nof.1, f32[80,80]{1,0:T(8,128)} %cs.1, ...), custom_call_target="tpu_custom_call" | custom-call | tf_op jit(solution)/shard_map/relax/pallas_call | solution.py:464
  53.0 0.0 copy-start
  53.0 2.0 %copy.17 = f32[80,4,2,1,128]{4,3,2,1,0:T(1,128)} copy(f32[80,4,2,1,128]{4,3,2,1,0:T(1,128)} %get-tuple-element.8) | data formatting | bytes 655360
  55.0 0.0 copy-done
  55.0 0.7 %copy.18 = f32[80,4,2,128]{3,2,1,0:T(2,128)} copy(f32[80,4,2,128]{3,2,1,0:T(2,128)S(1)} %bitcast.2) | data formatting | bytes 655360
Async XLA Ops:
  53.0 2.0 %copy-start = (f32[80,4,2,1,128]{4,3,2,1,0:T(1,128)S(1)}, f32[80,4,2,1,128]{4,3,2,1,0:T(1,128)}, u32[]{:S(2)}) copy-start(f32[80,4,2,1,128]{4,3,2,1,0:T(1,128)} %get-tuple-element.5) | copy-start | bytes 983044
where the time goes:
time: 55.8 us; the launch traced here: 55.7 us
  Pallas kernels  52.3 us (94%)
  local copies, waits for them, and re-layouts  2.7 us (5%)
  between operations  0.65 us (1%)
    pallas_call x1, Pallas kernels, per_device(): pl.pallas_call(body, out_shape=(out, out), in_specs=[hbm] * 13, out_specs...  52.3 us
    unnamed x4, local copies, waits for them, and re-layouts  2.7 us

commit v1 on v0

--- a/solution.py
+++ b/solution.py
@@ -45,8 +45,8 @@
     pse_ref, stf_ref, nof_ref, cs_ref, cn_ref, refl_ref, lam_ref, start_ref, length_ref, order_ref,
     u_buf, ul_buf, ur_buf, f_buf, spf_send, spl_recv, m2_send, m2l_recv, m2r_recv,
     e_send, e_recv, g_send, g_recv, y_send, y_recv,
-    pad_buf, da_buf, db_buf, f0_buf, f1_buf, inv_buf, a_buf, b_buf, d_buf, rel_buf, ls_buf,
-    loc_sem, out_sem, halo_send_sem, halo_recv_sem, tiny_send_sem, tiny_recv_sem,
+    pad_buf, da_buf, db_buf, f0_buf, f1_buf, inv_buf, a_buf, b_buf, d_buf, modal_buf,
+    loc_sem, halo_send_sem, halo_recv_sem, tiny_send_sem, tiny_recv_sem,
     e_sems, gs_sem, gr_sem, ys_sem, yr_sem,
 ):
     me = lax.axis_index("stream")
@@ -57,6 +57,22 @@
     sp_right = lax.rem(sp + 1, sp_count)
     st_left = lax.rem(me + count - 1, count)
     st_right = lax.rem(me + 1, count)
+
+    def peer_of(i):
+        return lax.rem(me + 1 + lax.rem(i + 26, count - 1), count)
+
+    g_recv[...] = jnp.zeros_like(g_recv)
+    barrier = pltpu.get_barrier_semaphore()
+    for side in (sp_left, sp_right):
+        pl.semaphore_signal(barrier, inc=1, device_id={"span": side}, device_id_type=MESH)
+
+    def greet(i, carry):
+        pl.semaphore_signal(
+            barrier, inc=1, device_id={"stream": peer_of(i)}, device_id_type=MESH
+        )
+        return carry
+
+    lax.fori_loop(0, count - 1, greet, 0)
 
     loads_u = [
         pltpu.make_async_copy(sol.at[:, rs // 2, rs % 2, 0, :], u_buf.at[rs], loc_sem.at[rs]) for rs in range(8)
@@ -80,19 +96,7 @@
         load.start()
     for load in loads_f:
         load.start()
-    g_recv[...] = jnp.zeros_like(g_recv)
-
-    barrier = pltpu.get_barrier_semaphore()
-    for side in (sp_left, sp_right):
-        pl.semaphore_signal(barrier, inc=1, device_id={"span": side}, device_id_type=MESH)
-
-    def greet(i, carry):
-        pl.semaphore_signal(
-            barrier, inc=1, device_id={"stream": lax.rem(me + i, count)}, device_id_type=MESH
-        )
-        return carry
-
-    lax.fori_loop(1, count, greet, 0)
+
 
     for load in loads_small[:4]:
         load.wait()
@@ -103,30 +107,6 @@
     pair_line = row // 64
     pick = jnp.where(lane == 2 * (row - 64 * pair_line) + pair_line, 1.0, 0.0).astype(BF16)
     perm = dot(pick, perm_t, 1, 1).astype(BF16)
-
-    for load in loads_u:
-        load.wait()
-    pl.semaphore_wait(barrier, count + 1)
-
-    halos = []
-    for c in range(2):
-        for k, (side, buf) in enumerate(((sp_right, ul_buf), (sp_left, ur_buf))):
-            halo = pltpu.make_async_remote_copy(
-                u_buf.at[pl.ds(4 * c, 4)],
-                buf.at[pl.ds(4 * c, 4)],
-                halo_send_sem.at[2 * c + k],
-                halo_recv_sem.at[2 * c + k],
-                device_id={"span": side},
-                device_id_type=MESH,
-            )
-            if c == 0 and k == 0:
-                spf_halo = pltpu.make_async_remote_copy(
-                    spf_send, spl_recv, tiny_send_sem.at[0], tiny_recv_sem.at[0],
-                    device_id={"span": sp_right}, device_id_type=MESH,
-                )
-                spf_halo.start()
-            halo.start()
-            halos.append(halo)
 
     for load in loads_small[4:]:
         load.wait()
@@ -158,6 +138,8 @@
     m1 = dot3(side_p * jnp.abs(lam_row), basis, 1, 1)
     m2 = dot3(side_p * lam_row, basis, 1, 1)
     small = jnp.concatenate([m1, m2, zt], axis=0)
+    for load in loads_u:
+        load.wait()
     state = jnp.concatenate([u_buf[rs] for rs in range(8)], axis=1)
     small_u = dot3(small, state)
 
@@ -169,6 +151,69 @@
         for r in range(4):
             m2_send[s, 8 * r : 8 * r + 8, :] = part(8, r, s)
         m2_send[s, 32:40, :] = jnp.broadcast_to(stf_ref[s : s + 1, :], (8, 128))
+    line_start = start_ref[...]
+    line_end = line_start + length_ref[...]
+
+    def masked(faces, pos):
+        return jnp.where((pos >= line_start) & (pos + 1 < line_end), faces, 0.0)
+
+    face = [masked(stf_ref[s : s + 1, :], 2 * me + s) for s in range(2)]
+    lane1 = iota((1, 128), 1)
+    normal_face = [jnp.where(lane1 < 127, nof_ref[s : s + 1, :], 0.0) for s in range(2)]
+    normal_left = [jnp.where(lane1 > 0, pltpu.roll(normal_face[s], 1, 1), 0.0) for s in range(2)]
+    span_face = [spf_send[s : s + 1, :] for s in range(2)]
+    local_t = jnp.concatenate([basis, dot3(cn_ref[...], basis, 0, 0)], axis=0)
+    outer_t = jnp.concatenate([dot3(cs_ref[...], basis, 0, 0), side_p, jnp.zeros((8, 128), F32)], axis=0)
+    pad_rows = jnp.zeros((32, 128), F32)
+    turned_t = jnp.transpose(jnp.concatenate([local_t, outer_t], axis=0))[:80]
+    local_weights = split(turned_t[:, 0:160])
+    outer_weights = split(jnp.transpose(jnp.concatenate([outer_t, pad_rows], axis=0))[:80, 0:96])
+
+    def apply(pair, rows):
+        high, low = split(rows)
+        both = dot(jnp.concatenate(pair, axis=0), high)
+        return both[:80] + (both[80:] + dot(pair[0], low))
+
+    for load in loads_f:
+        load.wait()
+    for c in range(2):
+        columns = []
+        for rs in range(4 * c, 4 * c + 4):
+            s = rs % 2
+            u = u_buf[rs]
+            columns.append(
+                jnp.concatenate(
+                    [
+                        f_buf[rs],
+                        normal_left[s] * pltpu.roll(u, 1, 1) + normal_face[s] * pltpu.roll(u, 127, 1),
+                    ],
+                    axis=0,
+                )
+            )
+        modal_buf[c] = apply(local_weights, jnp.concatenate(columns, axis=1))
+
+    pl.semaphore_wait(barrier, count + 1)
+
+    halos = []
+    for c in range(2):
+        for k, (side, buf) in enumerate(((sp_right, ul_buf), (sp_left, ur_buf))):
+            halo = pltpu.make_async_remote_copy(
+                u_buf.at[pl.ds(4 * c, 4)],
+                buf.at[pl.ds(4 * c, 4)],
+                halo_send_sem.at[2 * c + k],
+                halo_recv_sem.at[2 * c + k],
+                device_id={"span": side},
+                device_id_type=MESH,
+            )
+            if c == 0 and k == 0:
+                spf_halo = pltpu.make_async_remote_copy(
+                    spf_send, spl_recv, tiny_send_sem.at[0], tiny_recv_sem.at[0],
+                    device_id={"span": sp_right}, device_id_type=MESH,
+                )
+                spf_halo.start()
+            halo.start()
+            halos.append(halo)
+
     m2_halos = [
         pltpu.make_async_remote_copy(
             m2_send.at[1 - k], buf, tiny_send_sem.at[1 + k], tiny_recv_sem.at[1 + k],
@@ -179,17 +224,6 @@
     for halo in m2_halos:
         halo.start()
 
-    line_start = start_ref[...]
-    line_end = line_start + length_ref[...]
-
-    def masked(faces, pos):
-        return jnp.where((pos >= line_start) & (pos + 1 < line_end), faces, 0.0)
-
-    face = [masked(stf_ref[s : s + 1, :], 2 * me + s) for s in range(2)]
-    lane1 = iota((1, 128), 1)
-    normal_face = [jnp.where(lane1 < 127, nof_ref[s : s + 1, :], 0.0) for s in range(2)]
-    normal_left = [jnp.where(lane1 > 0, pltpu.roll(normal_face[s], 1, 1), 0.0) for s in range(2)]
-    span_face = [spf_send[s : s + 1, :] for s in range(2)]
     spf_halo.wait_recv()
     span_left = [spl_recv[s : s + 1, :] for s in range(2)]
     diag = [
@@ -220,7 +254,7 @@
 
     def send_all(src, dst, rows, send_sem, recv_sem):
         def one(i, carry):
-            peer = lax.rem(me + i, count)
+            peer = lax.rem(me + 1 + lax.rem(i * 26 + 26, count - 1), count)
             pltpu.make_async_remote_copy(
                 src.at[peer, pl.ds(0, rows)],
                 dst.at[me, pl.ds(0, rows)],
@@ -231,7 +265,7 @@
             ).start()
             return carry
 
-        lax.fori_loop(1, count, one, 0)
+        lax.fori_loop(0, count - 1, one, 0)
 
     def wait_all(buf, rows, sem):
         blocks = buf.at[pl.ds(0, 63), pl.ds(0, rows)]
@@ -240,15 +274,6 @@
     send_all(e_send, e_recv, 2, e_sems.at[0], e_sems.at[1])
     e_recv[me] = e_send[me]
 
-    weights_t = jnp.concatenate(
-        [basis, dot3(cs_ref[...], basis, 0, 0), dot3(cn_ref[...], basis, 0, 0), side_p, jnp.zeros((8, 128), F32)],
-        axis=0,
-    )
-    weights = jnp.transpose(weights_t)[:80]
-    weights_high, weights_low = split(weights)
-    weights_both = jnp.concatenate([weights_high, weights_low], axis=0)
-    for load in loads_f:
-        load.wait()
     for halo in m2_halos:
         halo.wait_recv()
     face_left = [masked(m2l_recv[32:33, :], 2 * me - 1), face[0]]
@@ -260,24 +285,19 @@
         for r in (2 * c, 2 * c + 1):
             for s in range(2):
                 rs = 2 * r + s
-                u = u_buf[rs]
                 before = m2l_recv[8 * r : 8 * r + 8, :] if s == 0 else part(8, r, 0)
                 after = part(8, r, 1) if s == 0 else m2r_recv[8 * r : 8 * r + 8, :]
                 columns.append(
                     jnp.concatenate(
                         [
-                            f_buf[rs],
                             span_left[s] * ul_buf[rs] + span_face[s] * ur_buf[rs],
-                            normal_left[s] * pltpu.roll(u, 1, 1) + normal_face[s] * pltpu.roll(u, 127, 1),
                             (face_left[s] + face[s]) * part(0, r, s) - face_left[s] * before - face[s] * after,
                             jnp.zeros((8, 128), F32),
                         ],
                         axis=0,
                     )
                 )
-        high, low = split(jnp.concatenate(columns, axis=1))
-        both = dot(weights_both, high)
-        modal = both[:80] + (both[80:] + dot(weights_high, low))
+        modal = modal_buf[c] + apply(outer_weights, jnp.concatenate(columns, axis=1))
         modal_high, modal_low = split(modal)
         g_flat = g_send.at[c].reshape(64 * 8, 128)
         for kg in range(5):
@@ -379,33 +399,26 @@
         both = dot(basis_both, high)
         return both[:80] + (both[80:] + dot(basis_high, low))
 
-    stores = []
     for c in range(2):
         wait_all(g_recv.at[c], 5, gr_sem.at[c])
 
-        def forward(p, d, c=c):
+        d = None
+        for p in range(32):
             near = g_recv[c, p]
             far = g_recv[c, 63 - p]
-            d = inv_buf[2 * p] * jnp.where(low8, near, far) + a_buf[2 * p] * d
+            even = inv_buf[2 * p] * jnp.where(low8, near, far)
+            d = even if d is None else even + a_buf[2 * p] * d
             d_buf[2 * p] = d
             odd = pltpu.roll(jnp.where(low8, far, near), 64, 1)
             d = inv_buf[2 * p + 1] * odd + a_buf[2 * p + 1] * d
             d_buf[2 * p + 1] = d
-            return d
-
-        d = lax.fori_loop(0, 32, forward, jnp.zeros((8, 128), F32))
-        y = (d + b_last * pltpu.roll(d, 64, 1)) * middle
-
-        def backward(i, y, c=c):
-            p = 31 - i
+        y = pltpu.roll((d + b_last * pltpu.roll(d, 64, 1)) * middle, 64, 1)
+        for p in reversed(range(32)):
             y_odd = d_buf[2 * p + 1] + b_buf[2 * p + 1] * y
-            y_even = d_buf[2 * p] + b_buf[2 * p] * y_odd
+            y = d_buf[2 * p] + b_buf[2 * p] * y_odd
             swapped = pltpu.roll(y_odd, 64, 1)
-            y_send[c, p] = jnp.where(low8, y_even, swapped)
-            y_send[c, 63 - p] = jnp.where(low8, swapped, y_even)
-            return y_even
-
-        lax.fori_loop(0, 32, backward, pltpu.roll(y, 64, 1))
+            y_send[c, p] = jnp.where(low8, y, swapped)
+            y_send[c, 63 - p] = jnp.where(low8, swapped, y)
         send_all(y_send.at[c], y_recv.at[c], 5, ys_sem.at[c], yr_sem.at[c])
         y_recv[c, me] = y_send[c, me]
         left = leave_modes(
@@ -417,11 +430,7 @@
         for r in range(2):
             for x in range(2):
                 at = (2 * c + r) * 2 + x
-                ls_buf[at] = left[:, (2 * r + x) * 128 : (2 * r + x) * 128 + 128]
-                stores.append(
-                    pltpu.make_async_copy(ls_buf.at[at], out_ls.at[:, 2 * c + r, x, 0, :], out_sem.at[at])
-                )
-                stores[-1].start()
+                out_ls[at] = left[:, (2 * r + x) * 128 : (2 * r + x) * 128 + 128]
     for c in range(2):
         wait_all(y_recv.at[c], 5, yr_sem.at[c])
         left = leave_modes(
@@ -430,11 +439,7 @@
         for r in range(2):
             for x in range(2):
                 at = (2 * c + r) * 2 + x
-                rel_buf[at] = left[:, (2 * r + x) * 128 : (2 * r + x) * 128 + 128]
-                stores.append(
-                    pltpu.make_async_copy(rel_buf.at[at], out_rel.at[:, 2 * c + r, x, 0, :], out_sem.at[8 + at])
-                )
-                stores[-1].start()
+                out_rel[at] = left[:, (2 * r + x) * 128 : (2 * r + x) * 128 + 128]
 
     spf_halo.wait_send()
     for halo in m2_halos:
@@ -445,14 +450,24 @@
     for c in range(2):
         wait_all(g_send.at[c], 5, gs_sem.at[c])
         wait_all(y_send.at[c], 5, ys_sem.at[c])
-    for store in stores:
-        store.wait()
+
+
+def store(rel, lines, out_rel, out_ls, sem):
+    copies = []
+    for at in range(8):
+        for k, (src, dst) in enumerate(((rel, out_rel), (lines, out_ls))):
+            copies.append(pltpu.make_async_copy(src.at[at], dst.at[:, at // 2, at % 2, 0, :], sem.at[8 * k + at]))
+    for copy in copies:
+        copy.start()
+    for copy in copies:
+        copy.wait()
 
 
 def per_device(
     solution, forcing, pseudo_shift, stream_faces, span_faces, normal_faces, coupling_span, coupling_normal,
     reflectors, eigenvalues, line_start, line_length, line_order,
 ):
+    vmem = pl.BlockSpec(memory_space=pltpu.VMEM)
     hbm = pl.BlockSpec(memory_space=pltpu.HBM)
     block = pltpu.VMEM((8, 80, 128), F32)
     per_peer = pltpu.VMEM((64, 8, 128), F32)
@@ -460,12 +475,12 @@
     two = pltpu.VMEM((2, 128), F32)
     line = pltpu.VMEM((1, 128), jnp.int32)
     dma = pltpu.SemaphoreType.DMA
-    out = jax.ShapeDtypeStruct((80, 4, 2, 1, 128), F32)
+    out = jax.ShapeDtypeStruct((8, 80, 128), F32)
     relaxed, line_states = pl.pallas_call(
         body,
         out_shape=(out, out),
         in_specs=[hbm] * 13,
-        out_specs=(hbm, hbm),
+        out_specs=(vmem, vmem),
         scratch_shapes=[
             two, two, two, pltpu.VMEM((80, 80), F32), pltpu.VMEM((80, 80), F32),
             pltpu.VMEM((8, 80), F32), pltpu.VMEM((1, 80), F32), line, line, line,
@@ -475,18 +490,29 @@
             per_peer, per_peer, pair_per_peer, pair_per_peer, pair_per_peer, pair_per_peer,
             pltpu.VMEM((16, 128), F32),
             pltpu.VMEM((64, 128), F32), pltpu.VMEM((64, 128), F32), pltpu.VMEM((64, 128), F32), pltpu.VMEM((72, 128), F32),
-            per_peer, per_peer, per_peer, per_peer, block, block,
-            dma((27,)), dma((16,)), dma((4,)), dma((4,)), dma((3,)), dma((3,)),
+            per_peer, per_peer, per_peer, per_peer, pltpu.VMEM((2, 80, 512), F32),
+            dma((27,)), dma((4,)), dma((4,)), dma((3,)), dma((3,)),
             dma((2,)), dma((2,)), dma((2,)), dma((2,)), dma((2,)),
         ],
         compiler_params=pltpu.CompilerParams(
-            collective_id=0, has_side_effects=True, vmem_limit_bytes=63 << 20
+            collective_id=0, has_side_effects=True, vmem_limit_bytes=48 << 20
         ),
         name="relax",
-    )(
+    )(*(pltpu.with_memory_space_constraint(a, pltpu.HBM) for a in (
         solution, forcing, pseudo_shift, stream_faces, span_faces, normal_faces,
         coupling_span, coupling_normal, reflectors, eigenvalues.reshape(1, 80), line_start, line_length, line_order,
-    )
+    )))
+    result = jax.ShapeDtypeStruct((80, 4, 2, 1, 128), F32)
+    anywhere = pl.BlockSpec(memory_space=pl.ANY)
+    relaxed, line_states = pl.pallas_call(
+        store,
+        out_shape=(result, result),
+        in_specs=[anywhere, anywhere],
+        out_specs=(hbm, hbm),
+        scratch_shapes=[dma((16,))],
+        compiler_params=pltpu.CompilerParams(vmem_limit_bytes=48 << 20),
+        name="relaxstore",
+    )(relaxed, line_states)
     return relaxed, line_states.reshape(80, 4, 2, 128)
 
 

time: 55.8 us -> 45.2 us (0.81)
  the two profiles are of different devices: /device:TPU:2 before, /device:TPU:1 now
where the time goes in v1:
time: 45.2 us; the launch traced here: 44.7 us
  Pallas kernels  44.1 us (98%)
  between operations  0.64 us (1%)
    pallas_call x1, Pallas kernels, per_device(): pl.pallas_call(body, out_shape=(out, out), in_specs=[hbm] * 13, out_specs...  43.1 us
    pallas_call x1, Pallas kernels, per_device(): pl.pallas_call(store, out_shape=(result, result), in_specs=[anywhere, any...  0.96 us

profile of v1, /device:TPU:1, one launch (start us, length us, event | category | flops | bytes accessed | tf_op | source)
XLA Modules:
  0.0 44.7 jit_solution(14158689498888809163)
XLA Ops:
  0.6 43.1 %relax.1 = (f32[8,80,128]{2,1,0:T(8,128)S(1)}, f32[8,80,128]{2,1,0:T(8,128)S(1)}) custom-call(f32[80,4,2,1,128]{4,3,2,1,0:T(1,128)} %sol.1, f32[80,4,2,1,128]{4,3,2,1,0:T(1,128)} %frc.1, f32[2,1,128]{2,1,0:T(1,128)} %pse.1, f32[2,1,128]{2,1,0:T(1,128)} %stf.1, f32[2,1,128]{2,1,0:T(1,128)} %spf.1, f32[2,1,128]{2,1,0:T(1,128)} %nof.1, f32[80,80]{1,0:T(8,128)} %cs.1, ...), custom_call_target="tpu_custom_call" | custom-call | tf_op jit(solution)/shard_map/relax/pallas_call | solution.py:479
  43.7 1.0 %relaxstore.1 = (f32[80,4,2,1,128]{4,3,2,1,0:T(1,128)}, f32[80,4,2,1,128]{4,3,2,1,0:T(1,128)}) custom-call(f32[8,80,128]{2,1,0:T(8,128)S(1)} %get-tuple-element.6.rel, f32[8,80,128]{2,1,0:T(8,128)S(1)} %get-tuple-element.7.lines), custom_call_target="tpu_custom_call" | custom-call | tf_op jit(solution)/shard_map/relaxstore/pallas_call | solution.py:507

commit v2 on v1

--- a/solution.py
+++ b/solution.py
@@ -58,8 +58,12 @@
     st_left = lax.rem(me + count - 1, count)
     st_right = lax.rem(me + 1, count)
 
+
     def peer_of(i):
-        return lax.rem(me + 1 + lax.rem(i + 26, count - 1), count)
+        jz, jy = i // 8, lax.rem(i, 8)
+        dy = 8 + (4 + ((jy + 1) // 2) * (1 - 2 * lax.rem(jy, 2)))
+        dz = 8 + (4 + ((jz + 1) // 2) * (1 - 2 * lax.rem(jz, 2)))
+        return lax.rem(me // 8 + dy, 8) * 8 + lax.rem(lax.rem(me, 8) + dz, 8)
 
     g_recv[...] = jnp.zeros_like(g_recv)
     barrier = pltpu.get_barrier_semaphore()
@@ -72,7 +76,7 @@
         )
         return carry
 
-    lax.fori_loop(0, count - 1, greet, 0)
+    lax.fori_loop(0, count - 1, greet, 0, unroll=9)
 
     loads_u = [
         pltpu.make_async_copy(sol.at[:, rs // 2, rs % 2, 0, :], u_buf.at[rs], loc_sem.at[rs]) for rs in range(8)
@@ -254,7 +258,7 @@
 
     def send_all(src, dst, rows, send_sem, recv_sem):
         def one(i, carry):
-            peer = lax.rem(me + 1 + lax.rem(i * 26 + 26, count - 1), count)
+            peer = peer_of(i)
             pltpu.make_async_remote_copy(
                 src.at[peer, pl.ds(0, rows)],
                 dst.at[me, pl.ds(0, rows)],
@@ -265,7 +269,7 @@
             ).start()
             return carry
 
-        lax.fori_loop(0, count - 1, one, 0)
+        lax.fori_loop(0, count - 1, one, 0, unroll=9)
 
     def wait_all(buf, rows, sem):
         blocks = buf.at[pl.ds(0, 63), pl.ds(0, rows)]
@@ -421,6 +425,7 @@
             y_send[c, 63 - p] = jnp.where(low8, swapped, y)
         send_all(y_send.at[c], y_recv.at[c], 5, ys_sem.at[c], yr_sem.at[c])
         y_recv[c, me] = y_send[c, me]
+    for c in range(2):
         left = leave_modes(
             y_send.at[c].reshape(64 * 8, 128),
             to_cell,

time: 45.2 us -> 43.6 us (0.965)
  Pallas kernels: 44.1 us -> 42.8 us
    pallas_call x1, Pallas kernels: 43.1 us -> 41.8 us  [per_device(): pl.pallas_call(body, out_shape=(out, out), in_specs=[hbm] * 13, out_specs...]
where the time goes in v2:
time: 43.6 us; the launch traced here: 43.4 us
  Pallas kernels  42.8 us (98%)
  between operations  0.64 us (1%)
    pallas_call x1, Pallas kernels, per_device(): pl.pallas_call(body, out_shape=(out, out), in_specs=[hbm] * 13, out_specs...  41.8 us
    pallas_call x1, Pallas kernels, per_device(): pl.pallas_call(store, out_shape=(result, result), in_specs=[anywhere, any...  0.96 us

profile of v2, /device:TPU:1, one launch (start us, length us, event | category | flops | bytes accessed | tf_op | source)
XLA Modules:
  0.0 43.4 jit_solution(3537548285407243837)
XLA Ops:
  0.6 41.8 %relax.1 = (f32[8,80,128]{2,1,0:T(8,128)S(1)}, f32[8,80,128]{2,1,0:T(8,128)S(1)}) custom-call(f32[80,4,2,1,128]{4,3,2,1,0:T(1,128)} %sol.1, f32[80,4,2,1,128]{4,3,2,1,0:T(1,128)} %frc.1, f32[2,1,128]{2,1,0:T(1,128)} %pse.1, f32[2,1,128]{2,1,0:T(1,128)} %stf.1, f32[2,1,128]{2,1,0:T(1,128)} %spf.1, f32[2,1,128]{2,1,0:T(1,128)} %nof.1, f32[80,80]{1,0:T(8,128)} %cs.1, ...), custom_call_target="tpu_custom_call" | custom-call | tf_op jit(solution)/shard_map/relax/pallas_call | solution.py:484
  42.5 1.0 %relaxstore.1 = (f32[80,4,2,1,128]{4,3,2,1,0:T(1,128)}, f32[80,4,2,1,128]{4,3,2,1,0:T(1,128)}) custom-call(f32[8,80,128]{2,1,0:T(8,128)S(1)} %get-tuple-element.6.rel, f32[8,80,128]{2,1,0:T(8,128)S(1)} %get-tuple-element.7.lines), custom_call_target="tpu_custom_call" | custom-call | tf_op jit(solution)/shard_map/relaxstore/pallas_call | solution.py:512

commit v3 on v2

--- a/solution.py
+++ b/solution.py
@@ -196,6 +196,15 @@
             )
         modal_buf[c] = apply(local_weights, jnp.concatenate(columns, axis=1))
 
+    lane64 = iota((64, 128), 1)
+    first_line = ((lane64 // 32) % 2) == 0
+    low_half = lane64 < 64
+    perm2 = jnp.concatenate([perm, perm], axis=1)
+    perm3 = jnp.concatenate([perm, perm, perm], axis=1)
+    h_rows = jnp.concatenate([part(16, r, s) for s in range(2) for l in range(2) for r in range(4)], axis=0)
+    e_flat = e_send.reshape(64 * 8, 128)
+    by_slot = dot(perm2, jnp.concatenate(split(h_rows), axis=1), 1, 1)
+    e_flat[pl.ds(0, 64, stride=8), :] = jnp.where(first_line, by_slot[:64], by_slot[64:])
     pl.semaphore_wait(barrier, count + 1)
 
     halos = []
@@ -235,12 +244,6 @@
         for s in range(2)
     ]
 
-    lane64 = iota((64, 128), 1)
-    first_line = ((lane64 // 32) % 2) == 0
-    low_half = lane64 < 64
-    perm2 = jnp.concatenate([perm, perm], axis=1)
-    perm3 = jnp.concatenate([perm, perm, perm], axis=1)
-    h_rows = jnp.concatenate([part(16, r, s) for s in range(2) for l in range(2) for r in range(4)], axis=0)
     c_rows = jnp.concatenate(
         [
             jnp.broadcast_to((diag, face)[q][s], (16, 128))
@@ -250,9 +253,6 @@
         ],
         axis=0,
     )
-    e_flat = e_send.reshape(64 * 8, 128)
-    by_slot = dot(perm2, jnp.concatenate(split(h_rows), axis=1), 1, 1)
-    e_flat[pl.ds(0, 64, stride=8), :] = jnp.where(first_line, by_slot[:64], by_slot[64:])
     by_slot = dot(perm3, jnp.concatenate(split3(c_rows), axis=1), 1, 1)
     e_flat[pl.ds(1, 64, stride=8), :] = jnp.where(first_line, by_slot[:64], by_slot[64:])
 
@@ -361,7 +361,7 @@
         inv = factor_step(2 * p, d_0, f_0, f_1, inv)
         return factor_step(2 * p + 1, d_1, f_1, f_2, inv)
 
-    lax.fori_loop(0, 32, factor, jnp.zeros((8, 128), F32))
+    lax.fori_loop(0, 32, factor, jnp.zeros((8, 128), F32), unroll=8)
     b_last = b_buf[63]
     middle = 1.0 / (1.0 - b_last * pltpu.roll(b_last, 64, 1))
 

time: 43.6 us -> 43.8 us (level)
  no operation moved by 1% of the time
where the time goes in v3:
time: 43.8 us; the launch traced here: 43.6 us
  Pallas kernels  43 us (98%)
  between operations  0.64 us (1%)
    pallas_call x1, Pallas kernels, per_device(): pl.pallas_call(body, out_shape=(out, out), in_specs=[hbm] * 13, out_specs...  42 us
    pallas_call x1, Pallas kernels, per_device(): pl.pallas_call(store, out_shape=(result, result), in_specs=[anywhere, any...  0.96 us

profile of v3, /device:TPU:1, one launch (start us, length us, event | category | flops | bytes accessed | tf_op | source)
XLA Modules:
  0.0 43.6 jit_solution(16988787879410956341)
XLA Ops:
  0.6 42.0 %relax.1 = (f32[8,80,128]{2,1,0:T(8,128)S(1)}, f32[8,80,128]{2,1,0:T(8,128)S(1)}) custom-call(f32[80,4,2,1,128]{4,3,2,1,0:T(1,128)} %sol.1, f32[80,4,2,1,128]{4,3,2,1,0:T(1,128)} %frc.1, f32[2,1,128]{2,1,0:T(1,128)} %pse.1, f32[2,1,128]{2,1,0:T(1,128)} %stf.1, f32[2,1,128]{2,1,0:T(1,128)} %spf.1, f32[2,1,128]{2,1,0:T(1,128)} %nof.1, f32[80,80]{1,0:T(8,128)} %cs.1, ...), custom_call_target="tpu_custom_call" | custom-call | tf_op jit(solution)/shard_map/relax/pallas_call | solution.py:484
  42.7 1.0 %relaxstore.1 = (f32[80,4,2,1,128]{4,3,2,1,0:T(1,128)}, f32[80,4,2,1,128]{4,3,2,1,0:T(1,128)}) custom-call(f32[8,80,128]{2,1,0:T(8,128)S(1)} %get-tuple-element.6.rel, f32[8,80,128]{2,1,0:T(8,128)S(1)} %get-tuple-element.7.lines), custom_call_target="tpu_custom_call" | custom-call | tf_op jit(solution)/shard_map/relaxstore/pallas_call | solution.py:512
